TPU v7x, 32 devices: a whole 2x2x4 slice. The times are simulated.
32 devices in a mesh: prow: 4 (over x, core), pcol: 8 (over z, y).
Axes of the slice: x: 2, y: 2, z: 4, core: 2. Of those that a mesh axis runs over, the one named last changes fastest.
Arguments:
- blocks: bfloat16 [20480, 128, 128], P(('prow', 'pcol')), may hold values from -0.078125 to 0.078125
- row_index: int32 [20480], P(('prow', 'pcol')), may hold values from 0 to 511, as said below
- col_index: int32 [20480], P(('prow', 'pcol')), may hold values from 0 to 511, as said below
- send_tiles: int32 [512], P(('prow', 'pcol')), may hold values from 0 to 511, as said below
- lighting: bfloat16 [65536, 384], P(('prow', 'pcol')), may hold values from -6 to 6
- albedo: float32 [3, 65536], P(None, ('pcol', 'prow')), may hold values from 0.2 to 0.95
- emission: bfloat16 [65536, 384], P(('pcol', 'prow')), may hold values from -4 to 4
Outputs:
- radiance: bfloat16 [65536, 384], P(('pcol', 'prow'))
Inputs may be any that keep to these rules, and one draw needn't show every extreme that they name: `send_tiles`: group g (the blocks of device g) lists 16 distinct tiles in increasing order: exactly 4 from each of the 4 ranges of 16 block rows starting at c * 64 + r * 16, r = 0 .. 3, where c = g % 8. `row_index`: each block's row is one of its group's listed tiles, each listed tile has at least one block, and a group's blocks are ordered by row; counts per tile are uneven. `col_index`: the blocks of group g have columns in (g // 8) * 128 to (g // 8 + 1) * 128 - 1; a pair of row and column may repeat, and then the blocks add.
All inputs are finite; a program needn't handle non-finite values.
Results may differ from a plain program's by a relative error of at most 0.008.
Values may be sent and summed in bfloat16 or wider, within the bound.
A program may use at most 192 MiB of HBM per device.

v0:
```python
import math
import jax
import jax.numpy as jnp
from jax import lax
from jax.sharding import PartitionSpec as P


def per_device(blocks, row_index, col_index, send_tiles, lighting, albedo, emission):
    tile_size = blocks.shape[1]
    col_width = lighting.shape[1]
    block_count = blocks.shape[0]
    list_count = send_tiles.shape[0]
    prow_count = lax.axis_size("prow")
    own_count = emission.shape[0] // tile_size
    strip_rows = own_count * prow_count
    prow_here = lax.axis_index("prow")
    pcol_here = lax.axis_index("pcol")
    slab = lax.all_gather(lighting, "pcol", axis=0, tiled=True)
    slab_count = slab.shape[0] // tile_size
    slab_flat = slab.reshape(slab_count, tile_size * col_width)
    local_cols = col_index - prow_here * slab_count
    slots = jnp.sum((send_tiles[None, :] < row_index[:, None]).astype(jnp.int32), axis=1)
    group_size = math.gcd(block_count, 64)
    group_total = block_count // group_size
    list_iota = jnp.arange(list_count, dtype=jnp.int32)

    def one_group(running, items):
        block_set, col_set, slot_set = items
        picked = jnp.take(slab_flat, col_set, axis=0).reshape(group_size, tile_size, col_width)
        product = jnp.einsum("gpq,gqk->gpk", block_set, picked, preferred_element_type=jnp.float32)
        placing = (list_iota[:, None] == slot_set[None, :]).astype(jnp.float32)
        summed_here = jnp.dot(
            placing,
            product.reshape(group_size, tile_size * col_width),
            precision=lax.Precision.HIGHEST,
            preferred_element_type=jnp.float32,
        )
        return (running + summed_here, None)

    start = jnp.zeros((list_count, tile_size * col_width), jnp.float32)
    summed, _ = lax.scan(
        one_group,
        start,
        (
            blocks.reshape(group_total, group_size, tile_size, tile_size),
            local_cols.reshape(group_total, group_size),
            slots.reshape(group_total, group_size),
        ),
    )
    part = summed.reshape(list_count, tile_size, col_width).astype(jnp.bfloat16)
    per_owner = list_count // prow_count
    arrived, arrived_ids = (
        lax.all_to_all(
            part.reshape(prow_count, per_owner, tile_size, col_width),
            "prow",
            split_axis=0,
            concat_axis=0,
            tiled=True,
        ),
        lax.all_to_all(
            send_tiles.reshape(prow_count, per_owner),
            "prow",
            split_axis=0,
            concat_axis=0,
            tiled=True,
        ),
    )
    owned_ids = arrived_ids.reshape(-1) - (pcol_here * strip_rows + prow_here * own_count)
    placing = (jnp.arange(own_count)[:, None] == owned_ids[None, :]).astype(jnp.bfloat16)
    gathered = jnp.einsum(
        "os,spk->opk",
        placing,
        arrived.reshape(list_count, tile_size, col_width),
        preferred_element_type=jnp.float32,
    )
    patch_count = own_count * tile_size
    colour_count = albedo.shape[0]
    lit = (
        gathered.reshape(patch_count, colour_count, col_width // colour_count)
        * jnp.transpose(albedo)[:, :, None]
    )
    return (lit.reshape(patch_count, col_width) + emission.astype(jnp.float32)).astype(jnp.bfloat16)


def solution(mesh):
    placed = (
        P(("prow", "pcol"), None, None),
        P(("prow", "pcol")),
        P(("prow", "pcol")),
        P(("prow", "pcol")),
        P(("prow", "pcol"), None),
        P(None, ("pcol", "prow")),
        P(("pcol", "prow"), None),
    )
    return jax.shard_map(
        per_device, mesh=mesh, in_specs=placed, out_specs=P(("pcol", "prow"), None), check_vma=False
    )
```

profile of v0, /device:TPU:0, one launch (start us, length us, event | category | flops | bytes accessed | tf_op | source)
XLA Modules:
  0.0 805.6 jit_solution(11871469207304912627)
XLA Ops:
  8.6 4.2 all-to-all-start
  14.4 174.3 %all-gather.2.cloned.1.call-done = bf16[16384,384]{1,0:T(8,128)(2,1)} async-done(((bf16[2048,384]{1,0:T(8,128)(2,1)}), bf16[16384,384]{1,0:T(8,128)(2,1)}) %all-gather.2.cloned.1.call-update) | async-done | bytes 12582928 | tf_op jit(solution)/shard_map/all_gather | solution.py:18
  188.7 17.2 %reshape.88 = bf16[128,49152]{1,0:T(8,128)(2,1)} reshape(bf16[16384,384]{1,0:T(8,128)(2,1)} %all-gather.2.cloned.1.call-done) | data formatting | bytes 25165824 | tf_op jit(solution)/shard_map/reshape | solution.py:20
  205.9 558.7 %while.11 = (s32[]{:T(128)}, f32[16,49152]{1,0:T(8,128)S(1)}, s32[10,64]{1,0:T(8,128)S(1)}, bf16[10,64,128,128]{3,2,1,0:T(8,128)(2,1)}, s32[10,64]{1,0:T(8,128)S...) while((s32[]{:T(128)}, f32[16,49152]{1,0:T(8,128)S(1)}, s32[10,64]{1,0:T(8,128)S(1)}, ...), condition=%wide.region_2.3_spmd.clone, body=%wide.region_1.2_spmd.clone.sunk | while | flops 1414007296 | bytes 102767336 | solution.py:41
  205.9 18.6 %gather_fusion = bf16[64,49152]{1,0:T(8,128)(2,1)} fusion(bf16[128,49152]{1,0:T(8,128)(2,1)} %get-tuple-element.136, s32[1024]{0:T(1024)S(1)} %pad_clamp_fusion.2), kind=kCustom, calls=%fused_computation.clone.clone.1 | custom fusion | bytes 12583168 | tf_op jit(solution)/shard_map/while/body/eval_jaxpr/jit(_take)/gather | solution.py:29
  224.6 4.2 copy.32
  230.2 7.9 fusion.28
  238.1 16.3 %copy.33 = f32[8,8,128,384]{3,1,2,0:T(8,128)} copy(f32[8,8,128,384]{3,2,1,0:T(8,128)} %bitcast.59) | data formatting | bytes 25165824 | tf_op jit(solution)/shard_map/while
  254.3 7.4 convolution_add_fusion.2
  261.8 18.6 %gather_fusion = bf16[64,49152]{1,0:T(8,128)(2,1)} fusion(bf16[128,49152]{1,0:T(8,128)(2,1)} %get-tuple-element.136, s32[1024]{0:T(1024)S(1)} %pad_clamp_fusion.2), kind=kCustom, calls=%fused_computation.clone.clone.1 | custom fusion | bytes 12583168 | tf_op jit(solution)/shard_map/while/body/eval_jaxpr/jit(_take)/gather | solution.py:29
  280.4 4.2 copy.32
  286.0 7.9 fusion.28
  293.9 16.3 %copy.33 = f32[8,8,128,384]{3,1,2,0:T(8,128)} copy(f32[8,8,128,384]{3,2,1,0:T(8,128)} %bitcast.59) | data formatting | bytes 25165824 | tf_op jit(solution)/shard_map/while
  310.2 7.4 convolution_add_fusion.2
  317.6 18.6 %gather_fusion = bf16[64,49152]{1,0:T(8,128)(2,1)} fusion(bf16[128,49152]{1,0:T(8,128)(2,1)} %get-tuple-element.136, s32[1024]{0:T(1024)S(1)} %pad_clamp_fusion.2), kind=kCustom, calls=%fused_computation.clone.clone.1 | custom fusion | bytes 12583168 | tf_op jit(solution)/shard_map/while/body/eval_jaxpr/jit(_take)/gather | solution.py:29
  341.9 7.9 fusion.28
  349.8 16.3 %copy.33 = f32[8,8,128,384]{3,1,2,0:T(8,128)} copy(f32[8,8,128,384]{3,2,1,0:T(8,128)} %bitcast.59) | data formatting | bytes 25165824 | tf_op jit(solution)/shard_map/while
  366.0 7.4 convolution_add_fusion.2
  373.5 18.6 %gather_fusion = bf16[64,49152]{1,0:T(8,128)(2,1)} fusion(bf16[128,49152]{1,0:T(8,128)(2,1)} %get-tuple-element.136, s32[1024]{0:T(1024)S(1)} %pad_clamp_fusion.2), kind=kCustom, calls=%fused_computation.clone.clone.1 | custom fusion | bytes 12583168 | tf_op jit(solution)/shard_map/while/body/eval_jaxpr/jit(_take)/gather | solution.py:29
  397.7 7.9 fusion.28
  405.6 16.3 %copy.33 = f32[8,8,128,384]{3,1,2,0:T(8,128)} copy(f32[8,8,128,384]{3,2,1,0:T(8,128)} %bitcast.59) | data formatting | bytes 25165824 | tf_op jit(solution)/shard_map/while
  421.9 7.4 convolution_add_fusion.2
  429.3 18.6 %gather_fusion = bf16[64,49152]{1,0:T(8,128)(2,1)} fusion(bf16[128,49152]{1,0:T(8,128)(2,1)} %get-tuple-element.136, s32[1024]{0:T(1024)S(1)} %pad_clamp_fusion.2), kind=kCustom, calls=%fused_computation.clone.clone.1 | custom fusion | bytes 12583168 | tf_op jit(solution)/shard_map/while/body/eval_jaxpr/jit(_take)/gather | solution.py:29
  453.6 7.9 fusion.28
  461.5 16.3 %copy.33 = f32[8,8,128,384]{3,1,2,0:T(8,128)} copy(f32[8,8,128,384]{3,2,1,0:T(8,128)} %bitcast.59) | data formatting | bytes 25165824 | tf_op jit(solution)/shard_map/while
  477.7 7.4 convolution_add_fusion.2
  485.2 18.6 %gather_fusion = bf16[64,49152]{1,0:T(8,128)(2,1)} fusion(bf16[128,49152]{1,0:T(8,128)(2,1)} %get-tuple-element.136, s32[1024]{0:T(1024)S(1)} %pad_clamp_fusion.2), kind=kCustom, calls=%fused_computation.clone.clone.1 | custom fusion | bytes 12583168 | tf_op jit(solution)/shard_map/while/body/eval_jaxpr/jit(_take)/gather | solution.py:29
  509.4 7.9 fusion.28
  517.3 16.3 %copy.33 = f32[8,8,128,384]{3,1,2,0:T(8,128)} copy(f32[8,8,128,384]{3,2,1,0:T(8,128)} %bitcast.59) | data formatting | bytes 25165824 | tf_op jit(solution)/shard_map/while
  533.6 7.4 convolution_add_fusion.2
  541.0 18.6 %gather_fusion = bf16[64,49152]{1,0:T(8,128)(2,1)} fusion(bf16[128,49152]{1,0:T(8,128)(2,1)} %get-tuple-element.136, s32[1024]{0:T(1024)S(1)} %pad_clamp_fusion.2), kind=kCustom, calls=%fused_computation.clone.clone.1 | custom fusion | bytes 12583168 | tf_op jit(solution)/shard_map/while/body/eval_jaxpr/jit(_take)/gather | solution.py:29
  565.3 7.9 fusion.28
  573.2 16.3 %copy.33 = f32[8,8,128,384]{3,1,2,0:T(8,128)} copy(f32[8,8,128,384]{3,2,1,0:T(8,128)} %bitcast.59) | data formatting | bytes 25165824 | tf_op jit(solution)/shard_map/while
  589.4 7.4 convolution_add_fusion.2
  596.9 18.6 %gather_fusion = bf16[64,49152]{1,0:T(8,128)(2,1)} fusion(bf16[128,49152]{1,0:T(8,128)(2,1)} %get-tuple-element.136, s32[1024]{0:T(1024)S(1)} %pad_clamp_fusion.2), kind=kCustom, calls=%fused_computation.clone.clone.1 | custom fusion | bytes 12583168 | tf_op jit(solution)/shard_map/while/body/eval_jaxpr/jit(_take)/gather | solution.py:29
  621.1 7.9 fusion.28
  629.0 16.3 %copy.33 = f32[8,8,128,384]{3,1,2,0:T(8,128)} copy(f32[8,8,128,384]{3,2,1,0:T(8,128)} %bitcast.59) | data formatting | bytes 25165824 | tf_op jit(solution)/shard_map/while
  645.3 7.4 convolution_add_fusion.2
  652.7 18.6 %gather_fusion = bf16[64,49152]{1,0:T(8,128)(2,1)} fusion(bf16[128,49152]{1,0:T(8,128)(2,1)} %get-tuple-element.136, s32[1024]{0:T(1024)S(1)} %pad_clamp_fusion.2), kind=kCustom, calls=%fused_computation.clone.clone.1 | custom fusion | bytes 12583168 | tf_op jit(solution)/shard_map/while/body/eval_jaxpr/jit(_take)/gather | solution.py:29
  677.0 7.9 fusion.28
  684.9 16.3 %copy.33 = f32[8,8,128,384]{3,1,2,0:T(8,128)} copy(f32[8,8,128,384]{3,2,1,0:T(8,128)} %bitcast.59) | data formatting | bytes 25165824 | tf_op jit(solution)/shard_map/while
  701.1 7.4 convolution_add_fusion.2
  708.6 18.6 %gather_fusion = bf16[64,49152]{1,0:T(8,128)(2,1)} fusion(bf16[128,49152]{1,0:T(8,128)(2,1)} %get-tuple-element.136, s32[1024]{0:T(1024)S(1)} %pad_clamp_fusion.2), kind=kCustom, calls=%fused_computation.clone.clone.1 | custom fusion | bytes 12583168 | tf_op jit(solution)/shard_map/while/body/eval_jaxpr/jit(_take)/gather | solution.py:29
  732.8 7.9 fusion.28
  740.7 16.3 %copy.33 = f32[8,8,128,384]{3,1,2,0:T(8,128)} copy(f32[8,8,128,384]{3,2,1,0:T(8,128)} %bitcast.59) | data formatting | bytes 25165824 | tf_op jit(solution)/shard_map/while
  757.0 7.4 convolution_add_fusion.2
  767.4 4.3 all-to-all-start.1
  775.2 16.6 %all-to-all-done.1 = bf16[4,4,128,384]{3,1,2,0:T(4,128)(2,1)} async-done(((bf16[4,4,128,384]{3,1,2,0:T(4,128)(2,1)}), bf16[4,4,128,384]{3,1,2,0:T(4,128)(2,1)}, u32[]{:S(2)}, u32[]{:S(2)}) %all-to-all-start.1) | async-done | bytes 1572896 | tf_op jit(solution)/shard_map/all_to_all | solution.py:53
  (85 shorter events, 64.2 us)
Async XLA Ops:
  6.5 182.2 %all-gather.2.cloned.1.call-start = ((), (), s32[]{:S(2)}) async-start(), calls=%async_computation.2 | async-start | bytes 14155776 | tf_op jit(solution)/shard_map/all_gather | solution.py:18
  8.6 758.8 %all-to-all-start = ((s32[4,1,4]{2,1,0:T(1,128)}), s32[4,1,4]{2,1,0:T(1,128)}, u32[]{:S(2)}, u32[]{:S(2)}) async-start(s32[4,1,4]{2,1,0:T(1,128)} %bitcast), calls=%async_computation | async-start | bytes 4096 | tf_op jit(solution)/shard_map/all_to_all | solution.py:60
  765.0 6.7 copy-start.2
  767.4 24.5 %all-to-all-start.1 = ((bf16[4,4,128,384]{3,1,2,0:T(4,128)(2,1)}), bf16[4,4,128,384]{3,1,2,0:T(4,128)(2,1)}, u32[]{:S(2)}, u32[]{:S(2)}) async-start(bf16[4,4,128,384]{3,1,2,0:T(4,128)(2,1)} %copy.23), calls=%async_computation.1 | async-start | bytes 3145728 | tf_op jit(solution)/shard_map/all_to_all | solution.py:53
  794.8 1.9 copy-start
  794.8 2.3 copy-start.1
Sparse Core Ops, SparseCore 0:
  9.5 179.1 all-gather.1
where the time goes:
time: 808 us; the launch traced here: 806 us
  local copies, waits for them, and re-layouts  420 us (52%)
  waiting for transfers between devices  192 us (24%)
  matrix products  154 us (19%)
  other arithmetic  17.8 us (2%)
  between operations  13.5 us (2%)
  starting transfers between devices  8.55 us (1%)
    while x20, local copies, waits for them, and re-layouts  204 us
    gather x10, local copies, waits for them, and re-layouts, one_group(): jnp.take(slab_flat, col_set, axis=0)  186 us
    all_gather x1, waiting for transfers between devices, per_device(): slab = lax.all_gather(lighting, 'pcol', axis=0, tiled=True)  174 us
    dot_general x10, matrix products, one_group(): jnp.einsum('gpq,gqk->gpk', block_set, picked, preferred_element_type=jnp....  79 us
    dot_general x10, matrix products, one_group(): jnp.dot(placing, product.reshape(group_size, tile_size * col_width), prec...  74.1 us
    reshape x1, local copies, waits for them, and re-layouts, per_device(): slab_flat = slab.reshape(slab_count, tile_size * col_width)  17.2 us
    all_to_all x1, waiting for transfers between devices, per_device(): lax.all_to_all(part.reshape(prow_count, per_owner, tile_size, col_width),...  16.6 us
  transfers between devices with their start and end apart: 3, of which 2 were waited for; matrix products, arithmetic and copies ran while one was open for 72% of the time, Pallas kernels for 0%

commit v1 on v0

--- a/solution.py
+++ b/solution.py
@@ -3,6 +3,12 @@
 import jax.numpy as jnp
 from jax import lax
 from jax.sharding import PartitionSpec as P
+
+
+def joined_along(blocks, dim):
+    shape = list(blocks.shape[1:])
+    shape[dim] *= blocks.shape[0]
+    return jnp.moveaxis(blocks, 0, dim).reshape(shape)
 
 
 def per_device(blocks, row_index, col_index, send_tiles, lighting, albedo, emission):
@@ -15,7 +21,19 @@
     strip_rows = own_count * prow_count
     prow_here = lax.axis_index("prow")
     pcol_here = lax.axis_index("pcol")
-    slab = lax.all_gather(lighting, "pcol", axis=0, tiled=True)
+    peers = lax.axis_size("pcol")
+    pairs = [(i, (i + 1) % peers) for i in range(peers)]
+    back = [(b, a) for a, b in pairs]
+    lower, upper = ([], [])
+    for step in range(peers - 1):
+        if step % 2 == 0:
+            lower.append(lax.ppermute(lower[-1] if lower else lighting, "pcol", pairs))
+        else:
+            upper.append(lax.ppermute(upper[-1] if upper else lighting, "pcol", back))
+    blocks_2 = jnp.stack([*lower[::-1], lighting, *upper])
+    shift = lax.axis_index("pcol") - len(lower)
+    blocks_2 = blocks_2[(jnp.arange(peers) - shift) % peers]
+    slab = joined_along(blocks_2, 0)
     slab_count = slab.shape[0] // tile_size
     slab_flat = slab.reshape(slab_count, tile_size * col_width)
     local_cols = col_index - prow_here * slab_count

time: 808 us -> 887 us (1.098)
  waiting for transfers between devices: 192 us -> 238 us
  local copies, waits for them, and re-layouts: 420 us -> 449 us
  starting transfers between devices: 8.55 us -> 25.2 us
  between operations: 13.5 us -> 0.17 us
    ppermute x0 -> x7, waiting for transfers between devices: none -> 222 us  [the longest x4 222 us: per_device(): lower.append(lax.ppermute(lower[-1] if lower else lighting, 'pcol', pairs))]
    all_gather x1 -> x0, waiting for transfers between devices: 174 us -> none  [per_device(): slab = lax.all_gather(lighting, 'pcol', axis=0, tiled=True)]
    another operation x0 -> x2, local copies, waits for them, and re-layouts: none -> 18.6 us  [the longest x1 17.2 us: per_device(): slab_flat = slab.reshape(slab_count, tile_size * col_width)]
    reshape x1 -> x0, local copies, waits for them, and re-layouts: 17.2 us -> none  [per_device(): slab_flat = slab.reshape(slab_count, tile_size * col_width)]
    ppermute x0 -> x7, starting transfers between devices: none -> 17.2 us  [the longest x3 9.15 us: per_device(): upper.append(lax.ppermute(upper[-1] if upper else lighting, 'pcol', back))]
    unnamed x7 -> x24, local copies, waits for them, and re-layouts: 1.58 us -> 18.2 us
    gather x0 -> x1, local copies, waits for them, and re-layouts: none -> 11.4 us  [per_device(): blocks_2 = blocks_2[(jnp.arange(peers) - shift) % peers]]
  transfers between devices with their start and end apart: 3 -> 9, of which waited for: 2 -> 5; matrix products, arithmetic and copies ran while one was open for 72% -> 69% of each run, Pallas kernels for 0% -> 0%
where the time goes in v1:
time: 887 us; the launch traced here: 885 us
  local copies, waits for them, and re-layouts  449 us (51%)
  waiting for transfers between devices  238 us (27%)
  matrix products  154 us (17%)
  starting transfers between devices  25.2 us (3%)
  other arithmetic  17.8 us (2%)
    ppermute x4, waiting for transfers between devices, per_device(): lower.append(lax.ppermute(lower[-1] if lower else lighting, 'pcol', pairs))  222 us
    while x20, local copies, waits for them, and re-layouts  205 us
    gather x10, local copies, waits for them, and re-layouts, one_group(): jnp.take(slab_flat, col_set, axis=0)  186 us
    dot_general x10, matrix products, one_group(): jnp.einsum('gpq,gqk->gpk', block_set, picked, preferred_element_type=jnp....  78.9 us
    dot_general x10, matrix products, one_group(): jnp.dot(placing, product.reshape(group_size, tile_size * col_width), prec...  74.1 us
    unnamed x24, local copies, waits for them, and re-layouts  18.2 us
  transfers between devices with their start and end apart: 9, of which 5 were waited for; matrix products, arithmetic and copies ran while one was open for 69% of the time, Pallas kernels for 0%

profile of v1, /device:TPU:0, one launch (start us, length us, event | category | flops | bytes accessed | tf_op | source)
XLA Modules:
  0.0 885.1 jit_solution(713574305366551290)
XLA Ops:
  3.0 37.6 %collective-permute-done = bf16[2048,384]{1,0:T(8,128)(2,1)S(1)} collective-permute-done((bf16[2048,384]{1,0:T(8,128)(2,1)}, bf16[2048,384]{1,0:T(8,128)(2,1)S(1)}, u32[]{:S(2)}, u32[]{:S(2)}) %collective-permute-start) | collective-permute-done | bytes 1572896 | tf_op jit(solution)/shard_map/ppermute | solution.py:30
  46.5 62.4 %collective-permute-done.1 = bf16[2048,384]{1,0:T(8,128)(2,1)S(1)} collective-permute-done((bf16[2048,384]{1,0:T(8,128)(2,1)S(1)}, bf16[2048,384]{1,0:T(8,128)(2,1)S(1)}, u32[]{:S(2)}, u32[]{:S(2)}) %collective-permute-start.1) | collective-permute-done | bytes 1572896 | tf_op jit(solution)/shard_map/ppermute | solution.py:30
  114.7 63.9 %collective-permute-done.2 = bf16[2048,384]{1,0:T(8,128)(2,1)} collective-permute-done((bf16[2048,384]{1,0:T(8,128)(2,1)S(1)}, bf16[2048,384]{1,0:T(8,128)(2,1)}, u32[]{:S(2)}, u32[]{:S(2)}) %collective-permute-start.2) | collective-permute-done | bytes 1572896 | tf_op jit(solution)/shard_map/ppermute | solution.py:30
  190.1 57.8 %collective-permute-done.3 = bf16[2048,384]{1,0:T(8,128)(2,1)} collective-permute-done((bf16[2048,384]{1,0:T(8,128)(2,1)}, bf16[2048,384]{1,0:T(8,128)(2,1)}, u32[]{:S(2)}, u32[]{:S(2)}) %collective-permute-start.3) | collective-permute-done | bytes 1572896 | tf_op jit(solution)/shard_map/ppermute | solution.py:30
  264.2 11.4 %gather_fusion.1 = bf16[8,2048,384]{2,1,0:T(8,128)(2,1)} fusion(bf16[8,2048,384]{2,1,0:T(8,128)(2,1)} %bitcast_dynamic-update-slice_fusion, s32[1024]{0:T(1024)S(1)} %pad_clamp_fusion.1), kind=kCustom, calls=%fused_computation.1 | custom fusion | bytes 25165856 | tf_op jit(solution)/shard_map/gather | solution.py:35
  275.5 17.2 %reshape_reshape.3 = bf16[128,49152]{1,0:T(8,128)(2,1)} reshape(bf16[8,2048,384]{2,1,0:T(8,128)(2,1)} %gather_fusion.1) | data formatting | bytes 25165824 | tf_op jit(solution)/shard_map/reshape;reshape | solution.py:38
  292.8 558.7 %while.11 = (s32[]{:T(128)}, f32[16,49152]{1,0:T(8,128)S(1)}, s32[10,64]{1,0:T(8,128)S(1)}, bf16[10,64,128,128]{3,2,1,0:T(8,128)(2,1)}, s32[10,64]{1,0:T(8,128)S...) while((s32[]{:T(128)}, f32[16,49152]{1,0:T(8,128)S(1)}, s32[10,64]{1,0:T(8,128)S(1)}, ...), condition=%wide.region_2.3_spmd.clone, body=%wide.region_1.2_spmd.clone.sunk | while | flops 1414007296 | bytes 102767336 | solution.py:59
  292.8 18.6 %gather_fusion = bf16[64,49152]{1,0:T(8,128)(2,1)} fusion(bf16[128,49152]{1,0:T(8,128)(2,1)} %get-tuple-element.136, s32[1024]{0:T(1024)S(1)} %pad_clamp_fusion.3), kind=kCustom, calls=%fused_computation.clone.clone.1 | custom fusion | bytes 12583168 | tf_op jit(solution)/shard_map/while/body/eval_jaxpr/jit(_take)/gather | solution.py:47
  317.0 7.9 fusion.30
  324.9 16.3 %copy.33 = f32[8,8,128,384]{3,1,2,0:T(8,128)} copy(f32[8,8,128,384]{3,2,1,0:T(8,128)} %bitcast.77) | data formatting | bytes 25165824 | tf_op jit(solution)/shard_map/while
  341.2 7.4 convolution_add_fusion.2
  348.6 18.6 %gather_fusion = bf16[64,49152]{1,0:T(8,128)(2,1)} fusion(bf16[128,49152]{1,0:T(8,128)(2,1)} %get-tuple-element.136, s32[1024]{0:T(1024)S(1)} %pad_clamp_fusion.3), kind=kCustom, calls=%fused_computation.clone.clone.1 | custom fusion | bytes 12583168 | tf_op jit(solution)/shard_map/while/body/eval_jaxpr/jit(_take)/gather | solution.py:47
  372.9 7.9 fusion.30
  380.8 16.3 %copy.33 = f32[8,8,128,384]{3,1,2,0:T(8,128)} copy(f32[8,8,128,384]{3,2,1,0:T(8,128)} %bitcast.77) | data formatting | bytes 25165824 | tf_op jit(solution)/shard_map/while
  397.0 7.4 convolution_add_fusion.2
  404.5 18.6 %gather_fusion = bf16[64,49152]{1,0:T(8,128)(2,1)} fusion(bf16[128,49152]{1,0:T(8,128)(2,1)} %get-tuple-element.136, s32[1024]{0:T(1024)S(1)} %pad_clamp_fusion.3), kind=kCustom, calls=%fused_computation.clone.clone.1 | custom fusion | bytes 12583168 | tf_op jit(solution)/shard_map/while/body/eval_jaxpr/jit(_take)/gather | solution.py:47
  428.7 7.9 fusion.30
  436.6 16.3 %copy.33 = f32[8,8,128,384]{3,1,2,0:T(8,128)} copy(f32[8,8,128,384]{3,2,1,0:T(8,128)} %bitcast.77) | data formatting | bytes 25165824 | tf_op jit(solution)/shard_map/while
  452.9 7.4 convolution_add_fusion.2
  460.3 18.6 %gather_fusion = bf16[64,49152]{1,0:T(8,128)(2,1)} fusion(bf16[128,49152]{1,0:T(8,128)(2,1)} %get-tuple-element.136, s32[1024]{0:T(1024)S(1)} %pad_clamp_fusion.3), kind=kCustom, calls=%fused_computation.clone.clone.1 | custom fusion | bytes 12583168 | tf_op jit(solution)/shard_map/while/body/eval_jaxpr/jit(_take)/gather | solution.py:47
  484.6 7.9 fusion.30
  492.5 16.3 %copy.33 = f32[8,8,128,384]{3,1,2,0:T(8,128)} copy(f32[8,8,128,384]{3,2,1,0:T(8,128)} %bitcast.77) | data formatting | bytes 25165824 | tf_op jit(solution)/shard_map/while
  508.7 7.4 convolution_add_fusion.2
  516.2 18.6 %gather_fusion = bf16[64,49152]{1,0:T(8,128)(2,1)} fusion(bf16[128,49152]{1,0:T(8,128)(2,1)} %get-tuple-element.136, s32[1024]{0:T(1024)S(1)} %pad_clamp_fusion.3), kind=kCustom, calls=%fused_computation.clone.clone.1 | custom fusion | bytes 12583168 | tf_op jit(solution)/shard_map/while/body/eval_jaxpr/jit(_take)/gather | solution.py:47
  540.4 7.9 fusion.30
  548.3 16.3 %copy.33 = f32[8,8,128,384]{3,1,2,0:T(8,128)} copy(f32[8,8,128,384]{3,2,1,0:T(8,128)} %bitcast.77) | data formatting | bytes 25165824 | tf_op jit(solution)/shard_map/while
  564.6 7.4 convolution_add_fusion.2
  572.0 18.6 %gather_fusion = bf16[64,49152]{1,0:T(8,128)(2,1)} fusion(bf16[128,49152]{1,0:T(8,128)(2,1)} %get-tuple-element.136, s32[1024]{0:T(1024)S(1)} %pad_clamp_fusion.3), kind=kCustom, calls=%fused_computation.clone.clone.1 | custom fusion | bytes 12583168 | tf_op jit(solution)/shard_map/while/body/eval_jaxpr/jit(_take)/gather | solution.py:47
  596.3 7.9 fusion.30
  604.2 16.3 %copy.33 = f32[8,8,128,384]{3,1,2,0:T(8,128)} copy(f32[8,8,128,384]{3,2,1,0:T(8,128)} %bitcast.77) | data formatting | bytes 25165824 | tf_op jit(solution)/shard_map/while
  620.4 7.4 convolution_add_fusion.2
  627.9 18.6 %gather_fusion = bf16[64,49152]{1,0:T(8,128)(2,1)} fusion(bf16[128,49152]{1,0:T(8,128)(2,1)} %get-tuple-element.136, s32[1024]{0:T(1024)S(1)} %pad_clamp_fusion.3), kind=kCustom, calls=%fused_computation.clone.clone.1 | custom fusion | bytes 12583168 | tf_op jit(solution)/shard_map/while/body/eval_jaxpr/jit(_take)/gather | solution.py:47
  652.1 7.9 fusion.30
  660.0 16.3 %copy.33 = f32[8,8,128,384]{3,1,2,0:T(8,128)} copy(f32[8,8,128,384]{3,2,1,0:T(8,128)} %bitcast.77) | data formatting | bytes 25165824 | tf_op jit(solution)/shard_map/while
  676.3 7.4 convolution_add_fusion.2
  683.8 18.6 %gather_fusion = bf16[64,49152]{1,0:T(8,128)(2,1)} fusion(bf16[128,49152]{1,0:T(8,128)(2,1)} %get-tuple-element.136, s32[1024]{0:T(1024)S(1)} %pad_clamp_fusion.3), kind=kCustom, calls=%fused_computation.clone.clone.1 | custom fusion | bytes 12583168 | tf_op jit(solution)/shard_map/while/body/eval_jaxpr/jit(_take)/gather | solution.py:47
  708.0 7.9 fusion.30
  715.9 16.3 %copy.33 = f32[8,8,128,384]{3,1,2,0:T(8,128)} copy(f32[8,8,128,384]{3,2,1,0:T(8,128)} %bitcast.77) | data formatting | bytes 25165824 | tf_op jit(solution)/shard_map/while
  732.1 7.4 convolution_add_fusion.2
  739.6 18.6 %gather_fusion = bf16[64,49152]{1,0:T(8,128)(2,1)} fusion(bf16[128,49152]{1,0:T(8,128)(2,1)} %get-tuple-element.136, s32[1024]{0:T(1024)S(1)} %pad_clamp_fusion.3), kind=kCustom, calls=%fused_computation.clone.clone.1 | custom fusion | bytes 12583168 | tf_op jit(solution)/shard_map/while/body/eval_jaxpr/jit(_take)/gather | solution.py:47
  763.8 7.9 fusion.30
  771.7 16.3 %copy.33 = f32[8,8,128,384]{3,1,2,0:T(8,128)} copy(f32[8,8,128,384]{3,2,1,0:T(8,128)} %bitcast.77) | data formatting | bytes 25165824 | tf_op jit(solution)/shard_map/while
  788.0 7.4 convolution_add_fusion.2
  795.5 18.6 %gather_fusion = bf16[64,49152]{1,0:T(8,128)(2,1)} fusion(bf16[128,49152]{1,0:T(8,128)(2,1)} %get-tuple-element.136, s32[1024]{0:T(1024)S(1)} %pad_clamp_fusion.3), kind=kCustom, calls=%fused_computation.clone.clone.1 | custom fusion | bytes 12583168 | tf_op jit(solution)/shard_map/while/body/eval_jaxpr/jit(_take)/gather | solution.py:47
  819.7 7.9 fusion.30
  827.6 16.3 %copy.33 = f32[8,8,128,384]{3,1,2,0:T(8,128)} copy(f32[8,8,128,384]{3,2,1,0:T(8,128)} %bitcast.77) | data formatting | bytes 25165824 | tf_op jit(solution)/shard_map/while
  843.8 7.4 convolution_add_fusion.2
  862.1 16.6 %all-to-all-done.1 = bf16[4,4,128,384]{3,1,2,0:T(4,128)(2,1)} async-done(((bf16[4,4,128,384]{3,1,2,0:T(4,128)(2,1)}), bf16[4,4,128,384]{3,1,2,0:T(4,128)(2,1)}, u32[]{:S(2)}, u32[]{:S(2)}) %all-to-all-start.1) | async-done | bytes 1572896 | tf_op jit(solution)/shard_map/all_to_all | solution.py:71
  (117 shorter events, 115.1 us)
Async XLA Ops:
  0.0 40.6 %collective-permute-start = (bf16[2048,384]{1,0:T(8,128)(2,1)}, bf16[2048,384]{1,0:T(8,128)(2,1)S(1)}, u32[]{:S(2)}, u32[]{:S(2)}) collective-permute-start(bf16[2048,384]{1,0:T(8,128)(2,1)} %param.13), channel_id=1, source_target_pairs={{0,1},{1,2},{2,3},{3,4},{4,5},{5,6},{6,7},{7,0},{8,9},{9,10},{10,1... | collective-permute-start | bytes 4718600 | tf_op jit(solution)/shard_map/ppermute | solution.py:30
  40.6 1.1 copy-start.3
  41.7 67.1 %collective-permute-start.1 = (bf16[2048,384]{1,0:T(8,128)(2,1)S(1)}, bf16[2048,384]{1,0:T(8,128)(2,1)S(1)}, u32[]{:S(2)}, u32[]{:S(2)}) collective-permute-start(bf16[2048,384]{1,0:T(8,128)(2,1)S(1)} %collective-permute-done), channel_id=1, source_target_pairs={{0,1},{1,2},{2,3},{3,4},{4,5},{5,6},{6,7},{7,0},{8,9},{9,10},{10,1... | collective-permute-start | bytes 4718600 | tf_op jit(solution)/shard_map/ppermute | solution.py:30
  41.7 70.7 %collective-permute-start.4 = (bf16[2048,384]{1,0:T(8,128)(2,1)}, bf16[2048,384]{1,0:T(8,128)(2,1)}, u32[]{:S(2)}, u32[]{:S(2)}) collective-permute-start(bf16[2048,384]{1,0:T(8,128)(2,1)} %param.13), channel_id=1, source_target_pairs={{1,0},{2,1},{3,2},{4,3},{5,4},{6,5},{7,6},{0,7},{9,8},{10,9},{11,1... | collective-permute-start | bytes 4718600 | tf_op jit(solution)/shard_map/ppermute | solution.py:32
  108.8 1.1 copy-start.5
  110.0 68.7 %collective-permute-start.2 = (bf16[2048,384]{1,0:T(8,128)(2,1)S(1)}, bf16[2048,384]{1,0:T(8,128)(2,1)}, u32[]{:S(2)}, u32[]{:S(2)}) collective-permute-start(bf16[2048,384]{1,0:T(8,128)(2,1)S(1)} %collective-permute-done.1), channel_id=1, source_target_pairs={{0,1},{1,2},{2,3},{3,4},{4,5},{5,6},{6,7},{7,0},{8,9},{9,10},{10,1... | collective-permute-start | bytes 4718600 | tf_op jit(solution)/shard_map/ppermute | solution.py:30
  112.5 75.5 %collective-permute-start.5 = (bf16[2048,384]{1,0:T(8,128)(2,1)}, bf16[2048,384]{1,0:T(8,128)(2,1)}, u32[]{:S(2)}, u32[]{:S(2)}) collective-permute-start(bf16[2048,384]{1,0:T(8,128)(2,1)} %collective-permute-done.4), channel_id=1, source_target_pairs={{1,0},{2,1},{3,2},{4,3},{5,4},{6,5},{7,6},{0,7},{9,8},{10,9},{11,1... | collective-permute-start | bytes 4718600 | tf_op jit(solution)/shard_map/ppermute | solution.py:32
  178.6 69.3 %collective-permute-start.3 = (bf16[2048,384]{1,0:T(8,128)(2,1)}, bf16[2048,384]{1,0:T(8,128)(2,1)}, u32[]{:S(2)}, u32[]{:S(2)}) collective-permute-start(bf16[2048,384]{1,0:T(8,128)(2,1)} %collective-permute-done.2), channel_id=1, source_target_pairs={{0,1},{1,2},{2,3},{3,4},{4,5},{5,6},{6,7},{7,0},{8,9},{9,10},{10,1... | collective-permute-start | bytes 4718600 | tf_op jit(solution)/shard_map/ppermute | solution.py:30
  182.5 671.8 %all-to-all-start = ((s32[4,1,4]{2,1,0:T(1,128)}), s32[4,1,4]{2,1,0:T(1,128)}, u32[]{:S(2)}, u32[]{:S(2)}) async-start(s32[4,1,4]{2,1,0:T(1,128)} %bitcast), calls=%async_computation | async-start | bytes 4096 | tf_op jit(solution)/shard_map/all_to_all | solution.py:78
  187.9 65.5 %copy-start.6 = (bf16[2048,384]{1,0:T(8,128)(2,1)S(1)}, bf16[2048,384]{1,0:T(8,128)(2,1)}, u32[]{:S(2)}) copy-start(bf16[2048,384]{1,0:T(8,128)(2,1)} %copy-done.5) | copy-start | bytes 4718596
  187.9 66.8 %copy-start.4 = (bf16[2048,384]{1,0:T(8,128)(2,1)S(1)}, bf16[2048,384]{1,0:T(8,128)(2,1)}, u32[]{:S(2)}) copy-start(bf16[2048,384]{1,0:T(8,128)(2,1)} %copy-done.3) | copy-start | bytes 4718596
  187.9 68.1 %copy-start.2 = (bf16[2048,384]{1,0:T(8,128)(2,1)S(1)}, bf16[2048,384]{1,0:T(8,128)(2,1)}, u32[]{:S(2)}) copy-start(bf16[2048,384]{1,0:T(8,128)(2,1)} %param.13) | copy-start | bytes 4718596
  187.9 74.9 %collective-permute-start.6 = (bf16[2048,384]{1,0:T(8,128)(2,1)}, bf16[2048,384]{1,0:T(8,128)(2,1)S(1)}, u32[]{:S(2)}, u32[]{:S(2)}) collective-permute-start(bf16[2048,384]{1,0:T(8,128)(2,1)} %collective-permute-done.5), channel_id=1, source_target_pairs={{1,0},{2,1},{3,2},{4,3},{5,4},{6,5},{7,6},{0,7},{9,8},{10,9},{11,1... | collective-permute-start | bytes 4718600 | tf_op jit(solution)/shard_map/ppermute | solution.py:32
  851.5 7.2 copy-start.7
  854.3 24.5 %all-to-all-start.1 = ((bf16[4,4,128,384]{3,1,2,0:T(4,128)(2,1)}), bf16[4,4,128,384]{3,1,2,0:T(4,128)(2,1)}, u32[]{:S(2)}, u32[]{:S(2)}) async-start(bf16[4,4,128,384]{3,1,2,0:T(4,128)(2,1)} %copy.23), calls=%async_computation.1 | async-start | bytes 3145728 | tf_op jit(solution)/shard_map/all_to_all | solution.py:71
  881.2 1.9 copy-start
  881.2 2.3 copy-start.1
